TPU v7x, 32 devices: a whole 2x2x4 slice. The times are simulated.
32 devices in a mesh: groups: 2 (over y), replica: 4 (over z), tensor: 2 (over x), sub: 2 (over core).
Axes of the slice: x: 2, y: 2, z: 4, core: 2. Of those that a mesh axis runs over, the one named last changes fastest.
Arguments:
- activations: bfloat16 [6144, 4096], P(('groups', 'replica', 'sub'), 'tensor'), parts along dimension 0, may hold values from -6 to 6
- row_voice_index: int32 [6144], P(('groups', 'replica', 'sub')), parts along dimension 0, may hold values from 0 to 51, as said below
- voice_slot_table: int32 [104], P('groups'), parts along dimension 0, may hold values from 0 to 51, as said below
- value_weight_matrix: bfloat16 [4096, 1024], P('tensor'), may hold values from -0.09375 to 0.09375
- adapter_down_weight: bfloat16 [104, 16, 4096], P(('groups', 'replica'), None, 'tensor'), parts along dimension 0, may hold values from -0.09375 to 0.09375
- adapter_up_weight: bfloat16 [104, 16, 1024], P(('groups', 'replica'), None, 'tensor'), parts along dimension 0, may hold values from -0.75 to 0.75
Outputs:
- values: bfloat16 [6144, 1024], P(('groups', 'replica', 'sub')), parts along dimension 0
There are 2 independent parts, one for each index of `groups`. A program takes and returns all parts, laid end to end along the dimension named above; an argument that names none is the same for every part. Nothing has to cross between parts.
Inputs may be any that keep to these rules, and one draw needn't show every extreme that they name: Every slot is named by exactly one voice; voice v's panels are row voice_slot_table[v] of adapter_down_weight and adapter_up_weight, and its owner is voice_slot_table[v] // 13. `row_voice_index`: in each aligned block of 384 rows (the rows of one device) at most 96 rows name voices of any one owner, and exactly 96 rows name voices of one owner.
All inputs are finite; a program needn't handle non-finite values.
Results may differ from a plain program's by a relative error of at most 0.004.
Values may be sent and summed in bfloat16 or wider, within the bound.
A program may use at most 64 MiB of HBM per device.

v0:
```python
import jax
import jax.numpy as jnp
from jax import lax
from jax.sharding import PartitionSpec as P

DELTA_GAIN = 2.0


def local(
    activations,
    row_voice_index,
    voice_slot_table,
    value_weight_matrix,
    adapter_down_weight,
    adapter_up_weight,
):
    row_count, feature_width = activations.shape
    owner_count = lax.axis_size("replica")
    resident_voices, rank_product, unused_item = adapter_down_weight.shape
    column_span = adapter_up_weight.shape[2]
    capacity = max(2, row_count // min(owner_count, 8))
    slot_of_row = jnp.take(voice_slot_table, row_voice_index)
    holder_position = slot_of_row // resident_voices
    local_slot = slot_of_row - holder_position * resident_voices
    owner_onehot = (
        holder_position[:, None] == jnp.arange(owner_count, dtype=jnp.int32)[None, :]
    ).astype(jnp.int32)
    position = jnp.sum(jnp.cumsum(owner_onehot, axis=0) * owner_onehot, axis=1) - 1
    destination = holder_position * capacity + position
    send_rows = (
        jnp.zeros((owner_count * capacity, feature_width), activations.dtype)
        .at[destination]
        .set(activations)
    )
    send_rows = send_rows.reshape(owner_count, capacity, feature_width)
    send_slots = jnp.full((owner_count * capacity,), -1, jnp.int32).at[destination].set(local_slot)
    send_slots = send_slots.reshape(owner_count, capacity)
    section_speaker = jnp.arange(resident_voices * rank_product, dtype=jnp.int32) // rank_product
    down_matrices = adapter_down_weight.reshape(resident_voices * rank_product, feature_width)
    expanding_factors = adapter_up_weight.reshape(resident_voices * rank_product, column_span)
    base_part = jnp.dot(activations, value_weight_matrix, preferred_element_type=jnp.float32)
    rows_in = lax.all_to_all(send_rows, "replica", split_axis=0, concat_axis=0, tiled=True)
    slots_in = lax.all_to_all(send_slots, "replica", split_axis=0, concat_axis=0, tiled=True)
    source_rows, count_of_slots, unused_item = rows_in.shape
    merged_tokens = rows_in.reshape(source_rows * count_of_slots, feature_width)
    flat_slots = slots_in.reshape(source_rows * count_of_slots)
    select_mask = flat_slots[:, None] == section_speaker[None, :]
    projected = lax.dot_general(
        merged_tokens, down_matrices, (((1,), (1,)), ((), ())), preferred_element_type=jnp.float32
    )
    partial_rank = (
        jnp.where(select_mask, projected, 0.0)
        .reshape(-1, resident_voices, rank_product)
        .sum(axis=1)
    )
    summed = lax.psum(partial_rank, "tensor")
    narrowed_hidden = summed.astype(jnp.bfloat16)
    widened_rows = jnp.where(
        select_mask, jnp.tile(narrowed_hidden, (1, resident_voices)), jnp.zeros((), jnp.bfloat16)
    )
    speaker_correction = DELTA_GAIN * jnp.dot(
        widened_rows, expanding_factors, preferred_element_type=jnp.float32
    )
    returned = lax.all_to_all(
        speaker_correction.reshape(source_rows, count_of_slots, column_span),
        "replica",
        split_axis=0,
        concat_axis=0,
        tiled=True,
    )
    own_delta = jnp.take(returned.reshape(owner_count * capacity, column_span), destination, axis=0)
    share_sum = lax.psum_scatter(base_part, "tensor", scatter_dimension=1, tiled=True)
    group_outputs = (share_sum + own_delta).astype(jnp.bfloat16)
    values = lax.all_gather(group_outputs, "tensor", axis=1, tiled=True)
    return values


def solution(mesh):
    in_specs = (
        P(("groups", "replica", "sub"), "tensor"),
        P(("groups", "replica", "sub")),
        P("groups"),
        P("tensor", None),
        P(("groups", "replica"), None, "tensor"),
        P(("groups", "replica"), None, "tensor"),
    )
    out_specs = P(("groups", "replica", "sub"), None)
    return jax.shard_map(local, mesh=mesh, in_specs=in_specs, out_specs=out_specs, check_vma=False)
```

profile of v0, /device:TPU:0, one launch (start us, length us, event | category | flops | bytes accessed | tf_op | source)
XLA Modules:
  0.0 155.8 jit_solution(7038279037841070843)
XLA Ops:
  6.5 0.0 copy-start
  6.5 2.1 %fusion.15 = (s32[1]{0:T(128)}, s32[1]{0:T(128)}, s32[1]{0:T(128)}, s32[1]{0:T(128)}, s32[1]{0:T(128)}, /*index=5*/s32[1]{0:T(128)}, s32[1]{0:T(128)}, s32[1]{0:...) fusion(s32[52]{0:T(128)} %param.8), kind=kLoop, calls=%fused_computation.44 | loop fusion | bytes 152 | tf_op jit(solution)/shard_map/jit(_take)/gather | solution.py:22
  8.6 2.1 %fusion.16 = (s32[1]{0:T(128)}, s32[1]{0:T(128)}, s32[1]{0:T(128)}, s32[1]{0:T(128)}, s32[1]{0:T(128)}, /*index=5*/s32[1]{0:T(128)}, s32[1]{0:T(128)}, s32[1]{0:...) fusion(s32[52]{0:T(128)} %param.8), kind=kLoop, calls=%fused_computation.45 | loop fusion | bytes 152 | tf_op jit(solution)/shard_map/jit(_take)/gather | solution.py:22
  10.7 1.8 %fusion.17 = (s32[1]{0:T(128)}, s32[1]{0:T(128)}, s32[1]{0:T(128)}, s32[1]{0:T(128)}, s32[1]{0:T(128)}, /*index=5*/s32[1]{0:T(128)}, s32[1]{0:T(128)}, s32[1]{0:...) fusion(s32[52]{0:T(128)} %param.8), kind=kLoop, calls=%fused_computation.46 | loop fusion | bytes 112 | tf_op jit(solution)/shard_map/jit(_take)/gather | solution.py:22
  12.5 33.1 %multiply_subtract_fusion = (s32[384]{0:T(512)S(1)}, s32[384]{0:T(512)S(1)}) fusion(s32[]{:T(128)} %bitcast.51, s32[]{:T(128)} %bitcast.50, s32[]{:T(128)} %bitcast.49, s32[]{:T(128)} %bitcast.48, s32[]{:T(128)} %bitcast.47, s32[]{:T(128)} %bitcast.46, s32[]{:T(128)} %bitcast.45, s32[]{:T(128)} %bitcast.44, s32[]{:T(128)} %bitcast.43, s32[]{:T(128)} %bitcast.42, ...), kind=kLoop, calls=%fused_computation.35 | loop fusion | flops 45696 | bytes 4816 | tf_op jit(solution)/shard_map/sub | solution.py:24
  45.7 1.2 reduce-window.6
  46.9 0.2 slice_reduce_fusion
  47.1 0.2 reduce-window.9
  47.3 0.1 add_bitcast_fusion
  47.4 2.9 %scatter_custom_fusion = s32[384]{0:T(512)S(1)} fusion(s32[384]{0:T(512)S(1)} %get-tuple-element.6, s32[384]{0:T(512)S(1)} %get-tuple-element.7, s32[]{:T(128)} %constant.69.clone.1), kind=kCustom, calls=%fused_computation.41 | custom fusion | bytes 1540 | tf_op jit(solution)/shard_map/scatter | solution.py:36
  50.3 0.7 all_to_all.12
  51.0 6.3 %all-to-all-start = ((s32[4,1,96]{2,1,0:T(1,128)}), s32[4,1,96]{2,1,0:T(1,128)S(1)}, u32[]{:S(2)}, u32[]{:S(2)}) async-start(s32[4,1,96]{2,1,0:T(1,128)} %all_to_all.12), calls=%async_computation.1 | async-start | bytes 4096 | tf_op jit(solution)/shard_map/all_to_all | solution.py:43
  57.3 5.0 %scatter_custom_fusion.1 = bf16[384,2048]{1,0:T(8,128)(2,1)} fusion(s32[384]{0:T(512)S(1)} %get-tuple-element.6, bf16[384,2048]{1,0:T(8,128)(2,1)} %param.6, bf16[]{:T(256)} %constant.76.clone.1), kind=kCustom, calls=%fused_computation.7 | custom fusion | bytes 1573376 | tf_op jit(solution)/shard_map/scatter | solution.py:33
  62.3 0.5 all-to-all-done
  62.8 4.6 %all-to-all-start.1 = ((bf16[4,96,2048]{2,1,0:T(8,128)(2,1)}), bf16[4,96,2048]{2,1,0:T(8,128)(2,1)S(1)}, u32[]{:S(2)}, u32[]{:S(2)}) async-start(bf16[4,96,2048]{2,1,0:T(8,128)(2,1)} %bitcast.54), calls=%async_computation.2 | async-start | bytes 3145728 | tf_op jit(solution)/shard_map/all_to_all | solution.py:42
  67.4 0.0 reduce-scatter.2.cloned.1.call-start
  67.4 5.6 %fusion.18 = f32[384,1024]{1,0:T(8,128)} fusion(bf16[384,2048]{1,0:T(8,128)(2,1)} %param.6, bf16[2048,1024]{1,0:T(8,128)(2,1)} %param.9), kind=kOutput, calls=%fused_computation.47 | convolution fusion | flops 1610612736 | bytes 7340032 | tf_op jit(solution)/shard_map/dot_general | solution.py:41
  73.0 0.0 reduce-scatter.2.cloned.1.call-update
  73.0 0.5 broadcast.383
  73.5 0.7 reduce.5
  74.2 0.1 eq.56
  74.3 29.5 %all-to-all-done.1 = bf16[4,96,2048]{2,1,0:T(8,128)(2,1)S(1)} async-done(((bf16[4,96,2048]{2,1,0:T(8,128)(2,1)}), bf16[4,96,2048]{2,1,0:T(8,128)(2,1)S(1)}, u32[]{:S(2)}, u32[]{:S(2)}) %all-to-all-start.1) | async-done | bytes 1572896 | tf_op jit(solution)/shard_map/all_to_all | solution.py:42
  103.8 0.0 copy-done
  103.8 0.0 copy-start.1
  103.8 0.7 convolution_select_fusion
  104.5 8.3 %psum.7 = bf16[384,16]{0,1:T(8,128)(2,1)S(1)} all-reduce(f32[384,16]{0,1:T(8,128)S(1)} %reduce_sum.19), channel_id=1, replica_groups=mesh['groups'=2,'replica'=4,'tensor'=2,'sub'=2] {'tensor'}, use_global_device_ids=true, to_apply=%region_7.8 | all-reduce | flops 6144 | bytes 36864 | tf_op jit(solution)/shard_map/psum | solution.py:56
  112.8 0.0 copy-done.1
  112.8 1.3 fusion
  114.1 3.5 %all-to-all-start.2 = ((f32[4,96,512]{2,1,0:T(8,128)}), f32[4,96,512]{2,1,0:T(8,128)S(1)}, u32[]{:S(2)}, u32[]{:S(2)}) async-start(f32[4,96,512]{2,1,0:T(8,128)} %bitcast.59), calls=%async_computation.3 | async-start | bytes 1572864 | tf_op jit(solution)/shard_map/all_to_all | solution.py:64
  117.6 17.5 %all-to-all-done.2 = f32[4,96,512]{2,1,0:T(8,128)S(1)} async-done(((f32[4,96,512]{2,1,0:T(8,128)}), f32[4,96,512]{2,1,0:T(8,128)S(1)}, u32[]{:S(2)}, u32[]{:S(2)}) %all-to-all-start.2) | async-done | bytes 786464 | tf_op jit(solution)/shard_map/all_to_all | solution.py:64
  135.2 1.6 %gather_fusion = f32[384,512]{1,0:T(8,128)S(1)} fusion(f32[384,512]{1,0:T(8,128)S(1)} %bitcast.84, s32[1024]{0:T(1024)S(1)} %pad_clamp_fusion), kind=kCustom, calls=%fused_computation | custom fusion | bytes 1574400 | tf_op jit(solution)/shard_map/jit(_take)/gather | solution.py:71
  136.8 0.0 reduce-scatter.2.cloned.1.call-done
  136.8 1.3 add_convert_fusion
  138.1 9.9 %all_gather.3 = bf16[384,1024]{1,0:T(8,128)(2,1)S(1)} all-gather(bf16[384,512]{1,0:T(8,128)(2,1)S(1)} %add_convert_fusion), channel_id=1, replica_groups=mesh['groups'=2,'replica'=4,'tensor'=2,'sub'=2] {'tensor'}, dimensions={1}, use_global_device_ids=true | all-gather | bytes 1179648 | tf_op jit(solution)/shard_map/all_gather | solution.py:74
  148.0 0.9 copy.10
  (7 shorter events, 0.1 us)
Async XLA Ops:
  6.5 97.2 %copy-start = (bf16[13,16,2048]{2,1,0:T(8,128)(2,1)S(1)}, bf16[13,16,2048]{2,1,0:T(8,128)(2,1)}, u32[]{:S(2)}) copy-start(bf16[13,16,2048]{2,1,0:T(8,128)(2,1)} %param.10) | copy-start | bytes 2555908
  51.0 11.8 %all-to-all-start = ((s32[4,1,96]{2,1,0:T(1,128)}), s32[4,1,96]{2,1,0:T(1,128)S(1)}, u32[]{:S(2)}, u32[]{:S(2)}) async-start(s32[4,1,96]{2,1,0:T(1,128)} %all_to_all.12), calls=%async_computation.1 | async-start | bytes 4096 | tf_op jit(solution)/shard_map/all_to_all | solution.py:43
  62.8 41.0 %all-to-all-start.1 = ((bf16[4,96,2048]{2,1,0:T(8,128)(2,1)}), bf16[4,96,2048]{2,1,0:T(8,128)(2,1)S(1)}, u32[]{:S(2)}, u32[]{:S(2)}) async-start(bf16[4,96,2048]{2,1,0:T(8,128)(2,1)} %bitcast.54), calls=%async_computation.2 | async-start | bytes 3145728 | tf_op jit(solution)/shard_map/all_to_all | solution.py:42
  67.4 69.4 %reduce-scatter.2.cloned.1.call-start = ((), (), s32[]{:S(2)}) async-start(), calls=%async_computation.4 | async-start | bytes 2359296 | tf_op jit(solution)/shard_map/reduce_scatter | solution.py:72
  103.8 9.1 %copy-start.1 = (bf16[13,16,512]{2,1,0:T(8,128)(2,1)S(1)}, bf16[13,16,512]{2,1,0:T(8,128)(2,1)}, u32[]{:S(2)}) copy-start(bf16[13,16,512]{2,1,0:T(8,128)(2,1)} %param.11) | copy-start | bytes 638980
  114.1 21.1 %all-to-all-start.2 = ((f32[4,96,512]{2,1,0:T(8,128)}), f32[4,96,512]{2,1,0:T(8,128)S(1)}, u32[]{:S(2)}, u32[]{:S(2)}) async-start(f32[4,96,512]{2,1,0:T(8,128)} %bitcast.59), calls=%async_computation.3 | async-start | bytes 1572864 | tf_op jit(solution)/shard_map/all_to_all | solution.py:64
Sparse Core Ops, SparseCore 0:
  73.1 27.5 reduce-scatter.1
where the time goes:
time: 157 us; the launch traced here: 156 us
  waiting for transfers between devices  47.5 us (30%)
  other arithmetic  36.6 us (23%)
  blocking collectives  18.2 us (12%)
  local copies, waits for them, and re-layouts  17.9 us (11%)
  starting transfers between devices  14.4 us (9%)
  between operations  13.5 us (9%)
  matrix products  7.6 us (5%)
    sub x1, other arithmetic, local(): local_slot = slot_of_row - holder_position * resident_voices  33.1 us
    all_to_all x1, waiting for transfers between devices, local(): lax.all_to_all(send_rows, 'replica', split_axis=0, concat_axis=0, tiled=T...  29.5 us
    all_to_all x1, waiting for transfers between devices, local(): lax.all_to_all(speaker_correction.reshape(source_rows, count_of_slots, co...  17.5 us
    all_gather x1, blocking collectives, local(): values = lax.all_gather(group_outputs, 'tensor', axis=1, tiled=True)  9.91 us
    psum x1, blocking collectives, local(): summed = lax.psum(partial_rank, 'tensor')  8.29 us
    all_to_all x1, starting transfers between devices, local(): lax.all_to_all(send_slots, 'replica', split_axis=0, concat_axis=0, tiled=...  6.32 us
    gather x3, local copies, waits for them, and re-layouts, local(): slot_of_row = jnp.take(voice_slot_table, row_voice_index)  5.99 us
    dot_general x1, matrix products, local(): jnp.dot(activations, value_weight_matrix, preferred_element_type=jnp.floa...  5.61 us
  transfers between devices with their start and end apart: 4, of which 3 were waited for; matrix products, arithmetic and copies ran while one was open for 10% of the time, Pallas kernels for 0%

commit v1 on v0

v1 whole, which is shorter than its diff:
```python
import functools

import jax
import jax.numpy as jnp
from jax import lax
from jax.experimental import pallas as pl
from jax.experimental.pallas import tpu as pltpu
from jax.sharding import PartitionSpec as P

DELTA_GAIN = 2.0
MESH = pl.DeviceIdType.MESH
TILE = 256
F32 = jnp.float32
BF16 = jnp.bfloat16


def kernel(
    n,
    t,
    voices,
    rank,
    voice,
    table,
    act,
    weight,
    down,
    up,
    out,
    act_v,
    w_v,
    pd,
    pu,
    xb,
    total,
    xr,
    slot_v,
    z_send,
    z_recv,
    sib_send,
    sib_recv,
    xu_send,
    xu_recv,
    sx_send,
    sx_recv,
    xb_send,
    xb_recv,
    xr_send,
    xr_recv,
    w_sem,
    loc_sem,
):
    rows, feat = act_v.shape
    width = w_v.shape[1]
    span = up.shape[1]
    panel = voices * rank
    tiles = width // TILE
    me = lax.axis_index("replica")
    mx = lax.axis_index("tensor")
    core = lax.axis_index("sub")
    hu, hd, qd = span // 2, feat // 2, feat // 4

    def peer(p):
        return lax.rem(mx + p, t)

    def slab(o):
        return pl.ds(pl.multiple_of(o * panel, 16), panel)

    def u_cols(k):
        return pl.ds(pl.multiple_of(k * hu, 128), hu)

    def d_cols(k, j):
        return pl.ds(pl.multiple_of(k * hd + j * qd, 128), qd)

    def piece(o, j, k):
        if j == 0:
            return pu.at[mx, slab(o), u_cols(k)]
        return pd.at[o, :, d_cols(k, j - 1)]

    def own_piece(j):
        if j == 0:
            return up.at[:, u_cols(core)]
        return down.at[:, d_cols(core, j - 1)]

    def z_copy(direction, o, j, own=False):
        return pltpu.make_async_remote_copy(
            src_ref=own_piece(j) if own else piece(o, j, core),
            dst_ref=piece(o, j, core),
            send_sem=z_send.at[(direction + 1) // 2, o, j],
            recv_sem=z_recv.at[o, j],
            device_id={"replica": me + direction},
            device_id_type=MESH,
        )

    def sib_copy(o, j, k):
        return pltpu.make_async_remote_copy(
            src_ref=piece(o, j, k),
            dst_ref=piece(o, j, k),
            send_sem=sib_send.at[o, j],
            recv_sem=sib_recv.at[o, j],
            device_id={"sub": 1 - core},
            device_id_type=MESH,
        )

    def xu_copy(o, p, own=False):
        return pltpu.make_async_remote_copy(
            src_ref=own_piece(0) if own else piece(o, 0, core),
            dst_ref=piece(o, 0, core),
            send_sem=xu_send.at[o, p],
            recv_sem=xu_recv.at[o, t - p],
            device_id={"tensor": peer(p)},
            device_id_type=MESH,
        )

    def xu_arrival(o, p, k, send, recv):
        where = pu.at[peer(p), slab(o), u_cols(k)]
        return pltpu.make_async_remote_copy(
            src_ref=where,
            dst_ref=where,
            send_sem=send.at[o, p],
            recv_sem=recv.at[o, p],
            device_id={"sub": 1 - core},
            device_id_type=MESH,
        )

    def b_cols(i):
        return pl.ds(pl.multiple_of(i * TILE, TILE), TILE)

    def xb_copy(i, p, owner):
        return pltpu.make_async_remote_copy(
            src_ref=xb.at[owner, :, b_cols(i)],
            dst_ref=xb.at[owner, :, b_cols(i)],
            send_sem=xb_send.at[i, p],
            recv_sem=xb_recv.at[i, t - p],
            device_id={"tensor": peer(p)},
            device_id_type=MESH,
        )

    def xr_copy(s, p, owner):
        return pltpu.make_async_remote_copy(
            src_ref=xr.at[s, owner],
            dst_ref=xr.at[s, owner],
            send_sem=xr_send.at[s, p],
            recv_sem=xr_recv.at[s, t - p],
            device_id={"tensor": peer(p)},
            device_id_type=MESH,
        )

    def w_copy(i):
        return pltpu.make_async_copy(weight.at[:, b_cols(i)], w_v.at[:, b_cols(i)], w_sem.at[i])

    barrier = pltpu.get_barrier_semaphore()

    def greet(device):
        pl.semaphore_signal(barrier, inc=1, device_id=device, device_id_type=MESH)

    act_copy = pltpu.make_async_copy(act, act_v, loc_sem.at[0])
    down_copy = pltpu.make_async_copy(down, pd.at[me], loc_sem.at[1])
    up_copy = pltpu.make_async_copy(up, pu.at[mx, slab(me)], loc_sem.at[2])
    greet({"sub": 1 - core})
    for p in range(1, t):
        greet({"tensor": peer(p)})
    pl.when(me > 0)(lambda: greet({"replica": me - 1}))
    pl.when(me < n - 1)(lambda: greet({"replica": me + 1}))
    act_copy.start()
    for i in range(tiles):
        w_copy(i).start()
    down_copy.start()
    up_copy.start()
    ends = (me == 0).astype(jnp.int32) + (me == n - 1).astype(jnp.int32)
    pl.semaphore_wait(barrier, t + 2 - ends)

    for j in range(3):
        pl.when(me > 0)(lambda: z_copy(-1, me, j, True).start())
        pl.when(me < n - 1)(lambda: z_copy(1, me, j, True).start())
    for p in range(1, t):
        xu_copy(me, p, True).start()

    act_copy.wait()

    def base_tile(i, carry):
        w_copy(i).wait()
        part = jnp.dot(act_v[...], w_v[:, b_cols(i)], preferred_element_type=F32)
        xb[mx, :, b_cols(i)] = part.astype(BF16)
        for p in range(1, t):
            xb_copy(i, p, mx).start()
        return carry

    lax.fori_loop(0, tiles, base_tile, 0)

    row_voice = voice[...]

    def slot_step(v, slot):
        return jnp.where(row_voice == v, table[v], slot)

    slot_v[...] = lax.fori_loop(0, table.shape[0], slot_step, jnp.zeros_like(row_voice))

    def mask_of(o):
        section = lax.broadcasted_iota(jnp.int32, (panel, rows), 0) // rank
        return section == (slot_v[...] - o * voices)

    def project(o):
        made = lax.dot_general(
            pd[o], act_v[...], (((1,), (1,)), ((), ())), preferred_element_type=F32
        )
        kept = jnp.where(mask_of(o), made, 0.0)
        return kept.reshape(voices, rank, rows).sum(axis=0)

    def send_rank(s):
        for p in range(1, t):
            xr_copy(s, p, mx).start()

    def settle_owner(o, narrowed):
        for p in range(1, t):
            xu_arrival(o, p, core, xu_send, xu_recv).wait_recv()
            xu_arrival(o, p, core, sx_send, sx_recv).start()
        wide = jnp.where(mask_of(o), jnp.tile(narrowed, (voices, 1)), jnp.zeros((), BF16))
        for p in range(1, t):
            xu_arrival(o, p, 1 - core, sx_send, sx_recv).wait_recv()
        for x in range(t):
            total[:, x * span : (x + 1) * span] += lax.dot_general(
                wide, pu[x, slab(o)], (((0,), (0,)), ((), ())), preferred_element_type=F32
            )

    def rank_sum(s):
        for p in range(1, t):
            xr_copy(s, p, peer(p)).wait_recv()
        acc = xr[s, 0]
        for x in range(1, t):
            acc = acc + xr[s, x]
        return (DELTA_GAIN * acc.astype(BF16).astype(F32)).astype(BF16)

    def both(s, act_on):
        pl.when(me - s >= 0)(lambda: act_on(me - s, 1))
        pl.when(me + s < n)(lambda: act_on(me + s, -1))

    def settle(s):
        narrowed = rank_sum(s)
        both(s, lambda o, direction: settle_owner(o, narrowed))

    def onward(direction):
        return (me + direction >= 0) & (me + direction < n)

    total[...] = jnp.zeros_like(total)
    down_copy.wait()
    up_copy.wait()
    xr[0, mx] = project(me)
    send_rank(0)

    def step(s, carry):
        for j in range(3):

            def take(o, direction):
                z_copy(direction, o, j).wait_recv()
                pl.when(onward(direction))(lambda: z_copy(direction, o, j).start())
                sib_copy(o, j, core).start()
                if j == 0:
                    for p in range(1, t):
                        xu_copy(o, p).start()

            both(s, take)
        xr[s, mx] = jnp.zeros((rank, rows), F32)

        def work(o, direction):
            for j in range(3):
                sib_copy(o, j, 1 - core).wait_recv()
            xr[s, mx] += project(o)

        both(s, work)
        send_rank(s)

        @pl.when(s == 1)
        def _():
            settle_owner(me, rank_sum(0))

        @pl.when(s > 1)
        def _():
            settle(s - 1)

        return carry

    lax.fori_loop(1, n, step, 0)
    settle(n - 1)

    def base_wait(i, carry):
        for p in range(1, t):
            xb_copy(i, p, peer(p)).wait_recv()
        acc = total[:, b_cols(i)]
        for x in range(t):
            acc = acc + xb[x, :, b_cols(i)].astype(F32)
        out[:, b_cols(i)] = acc.astype(BF16)
        for p in range(1, t):
            xb_copy(i, p, mx).wait_send()
        return carry

    lax.fori_loop(0, tiles, base_wait, 0)

    for j in range(3):
        pl.when(me > 0)(lambda: z_copy(-1, me, j, True).wait_send())
        pl.when(me < n - 1)(lambda: z_copy(1, me, j, True).wait_send())
    for p in range(1, t):
        xu_copy(me, p, True).wait_send()
        xu_arrival(me, p, core, sx_send, sx_recv).wait_send()
        xr_copy(0, p, mx).wait_send()

    def drain(s, carry):
        def sent(o, direction):
            for j in range(3):
                pl.when(onward(direction))(lambda: z_copy(direction, o, j).wait_send())
                sib_copy(o, j, core).wait_send()
            for p in range(1, t):
                xu_copy(o, p).wait_send()
                xu_arrival(o, p, core, sx_send, sx_recv).wait_send()

        both(s, sent)
        for p in range(1, t):
            xr_copy(s, p, mx).wait_send()
        return carry

    lax.fori_loop(1, n, drain, 0)


def local(n, t, activations, row_voice, slot_table, weight, down, up):
    rows, feat = activations.shape
    voices, rank, span = up.shape
    width = weight.shape[1]
    panel = voices * rank
    any_spec = pl.BlockSpec(memory_space=pl.ANY)
    dma = pltpu.SemaphoreType.DMA
    return pl.pallas_call(
        functools.partial(kernel, n, t, voices, rank),
        out_shape=jax.ShapeDtypeStruct((rows, width), BF16),
        in_specs=[
            pl.BlockSpec(memory_space=pltpu.VMEM),
            pl.BlockSpec(memory_space=pltpu.SMEM),
            any_spec,
            any_spec,
            any_spec,
            any_spec,
        ],
        out_specs=pl.BlockSpec(memory_space=pltpu.VMEM),
        scratch_shapes=[
            pltpu.VMEM((rows, feat), BF16),
            pltpu.VMEM((feat, width), BF16),
            pltpu.VMEM((n, panel, feat), BF16),
            pltpu.VMEM((t, n * panel, span), BF16),
            pltpu.VMEM((t, rows, width), BF16),
            pltpu.VMEM((rows, width), F32),
            pltpu.VMEM((n, t, rank, rows), F32),
            pltpu.VMEM((1, rows), jnp.int32),
            dma((2, n, 3)),
            dma((n, 3)),
            dma((n, 3)),
            dma((n, 3)),
            dma((n, t)),
            dma((n, t)),
            dma((n, t)),
            dma((n, t)),
            dma((width // TILE, t)),
            dma((width // TILE, t)),
            dma((n, t)),
            dma((n, t)),
            dma((width // TILE,)),
            dma((3,)),
        ],
        compiler_params=pltpu.CompilerParams(
            collective_id=0, has_side_effects=True, vmem_limit_bytes=56 * 1024 * 1024
        ),
    )(
        row_voice.reshape(1, rows),
        slot_table,
        activations,
        weight,
        down.reshape(panel, feat),
        up.reshape(panel, span),
    )


def solution(mesh):
    in_specs = (
        P(("groups", "replica", "sub"), "tensor"),
        P(("groups", "replica", "sub")),
        P("groups"),
        P("tensor", None),
        P(("groups", "replica"), None, "tensor"),
        P(("groups", "replica"), None, "tensor"),
    )
    out_specs = P(("groups", "replica", "sub"), None)
    body = functools.partial(local, mesh.shape["replica"], mesh.shape["tensor"])
    return jax.shard_map(body, mesh=mesh, in_specs=in_specs, out_specs=out_specs, check_vma=False)
```

time: 157 us -> 52.9 us (0.34)
  Pallas kernels: 0 us -> 48.8 us
  waiting for transfers between devices: 47.5 us -> 0 us
  other arithmetic: 36.6 us -> 0 us
  blocking collectives: 18.2 us -> 0 us
  local copies, waits for them, and re-layouts: 17.9 us -> 3.31 us
  starting transfers between devices: 14.4 us -> 0 us
  between operations: 13.5 us -> 0.01 us
  matrix products: 7.6 us -> 0 us
    pallas_call x0 -> x1, Pallas kernels: none -> 48.8 us  [local(): pl.pallas_call(functools.partial(kernel, n, t, voices, rank), out_shape=j...]
    all_to_all x3 -> x0, waiting for transfers between devices: 47.5 us -> none  [the longest x1 29.5 us: local(): lax.all_to_all(send_rows, 'replica', split_axis=0, concat_axis=0, tiled=T...]
    sub x1 -> x0, other arithmetic: 33.1 us -> none  [local(): local_slot = slot_of_row - holder_position * resident_voices]
    all_to_all x3 -> x0, starting transfers between devices: 14.4 us -> none  [the longest x1 6.32 us: local(): lax.all_to_all(send_slots, 'replica', split_axis=0, concat_axis=0, tiled=...]
    all_gather x1 -> x0, blocking collectives: 9.91 us -> none  [local(): values = lax.all_gather(group_outputs, 'tensor', axis=1, tiled=True)]
    psum x1 -> x0, blocking collectives: 8.29 us -> none  [local(): summed = lax.psum(partial_rank, 'tensor')]
    scatter x2 -> x0, local copies, waits for them, and re-layouts: 7.89 us -> none  [the longest x1 4.97 us: local(): send_rows = jnp.zeros((owner_count * capacity, feature_width), activation...]
    gather x4 -> x0, local copies, waits for them, and re-layouts: 7.61 us -> none  [the longest x3 5.99 us: local(): slot_of_row = jnp.take(voice_slot_table, row_voice_index)]
  transfers between devices with their start and end apart: 4 -> 0, of which waited for: 3 -> 0; matrix products, arithmetic and copies ran while one was open for 10% -> 0% of each run, Pallas kernels for 0% -> 0%
where the time goes in v1:
time: 52.9 us; the launch traced here: 52.1 us
  Pallas kernels  48.8 us (92%)
  local copies, waits for them, and re-layouts  3.31 us (6%)
    pallas_call x1, Pallas kernels, local(): pl.pallas_call(functools.partial(kernel, n, t, voices, rank), out_shape=j...  48.8 us
    unnamed x1, local copies, waits for them, and re-layouts  2.06 us
    reshape x1, local copies, waits for them, and re-layouts, local(): row_voice.reshape(1, rows)  1.24 us

profile of v1, /device:TPU:0, one launch (start us, length us, event | category | flops | bytes accessed | tf_op | source)
XLA Modules:
  0.0 52.1 jit_solution(17339620276869934512)
XLA Ops:
  0.0 1.2 %reshape.9.voice = s32[1,384]{1,0:T(1,128)} reshape(s32[384]{0:T(512)} %param.7) | data formatting | bytes 3072 | tf_op jit(solution)/shard_map/reshape | solution.py:369
  1.2 48.8 %shard_map.64 = bf16[384,1024]{1,0:T(8,128)(2,1)} custom-call(s32[1,384]{1,0:T(1,128)} %reshape.9.voice, s32[52]{0:T(128)} %table.1, bf16[384,2048]{1,0:T(8,128)(2,1)} %act.1, bf16[2048,1024]{1,0:T(8,128)(2,1)} %weight.1, bf16[208,2048]{1,0:T(8,128)(2,1)} %bitcast.2, bf16[208,512]{1,0:T(8,128)(2,1)} %bitcast.3), custom_call_target="tpu_custom_call" | custom-call | tf_op jit(solution)/shard_map/pallas_call | solution.py:329
  50.0 2.1 %copy.8 = bf16[384,1024]{1,0:T(8,128)(2,1)} copy(bf16[384,1024]{1,0:T(8,128)(2,1)} %shard_map.64) | data formatting | bytes 1572864

commit v2 on v1

v2 whole, which is shorter than its diff:
```python
import functools

import jax
import jax.numpy as jnp
from jax import lax
from jax.experimental import pallas as pl
from jax.experimental.pallas import tpu as pltpu
from jax.sharding import PartitionSpec as P

DELTA_GAIN = 2.0
MESH = pl.DeviceIdType.MESH
TILE = 256
PARTS = 4
F32 = jnp.float32
BF16 = jnp.bfloat16


def kernel(
    n,
    t,
    voices,
    rank,
    cap,
    voice,
    table,
    act,
    weight,
    down,
    up,
    out,
    act_v,
    w_v,
    pd,
    pu,
    xb,
    total,
    xr,
    slot_v,
    made_v,
    perm_v,
    rows_out,
    tags_out,
    rows_in,
    tags_in,
    back_out,
    back_in,
    z_send,
    z_recv,
    sib_send,
    sib_recv,
    xu_send,
    xu_recv,
    sx_send,
    sx_recv,
    xb_send,
    xb_recv,
    xr_send,
    xr_recv,
    w_sem,
    loc_sem,
    trade_send,
    trade_recv,
):
    rows, feat = act_v.shape
    width = w_v.shape[1]
    span = up.shape[1]
    panel = voices * rank
    tile = min(TILE, span)
    tiles = width // tile
    me = lax.axis_index("replica")
    mx = lax.axis_index("tensor")
    core = lax.axis_index("sub")
    hu, hd, qd = span // 2, feat // 2, feat // (2 * PARTS)
    pieces = PARTS + 1
    trade = n >= 4
    is_end = ((me == 0) | (me == n - 1)) if trade else (me < 0)
    is_host = ((me == 1) | (me == n - 2)) if trade else (me < 0)
    inward = jnp.where(me == 0, 1, -1)
    outward = jnp.where(me == 1, -1, 1)
    lanes = perm_v.shape[0]

    def peer(p):
        return lax.rem(mx + p, t)

    def slab(o):
        return pl.ds(pl.multiple_of(o * panel, 16), panel)

    def u_cols(k):
        return pl.ds(pl.multiple_of(k * hu, 128), hu)

    def d_cols(k, j):
        return pl.ds(pl.multiple_of(k * hd + (j - 1) * qd, 128), qd)

    def piece(o, j, k):
        if j == 0:
            return pu.at[mx, slab(o), u_cols(k)]
        return pd.at[o, :, d_cols(k, j)]

    def own_piece(j):
        if j == 0:
            return up.at[:, u_cols(core)]
        return down.at[:, d_cols(core, j)]

    def z_copy(direction, o, j, own=False):
        return pltpu.make_async_remote_copy(
            src_ref=own_piece(j) if own else piece(o, j, core),
            dst_ref=piece(o, j, core),
            send_sem=z_send.at[(direction + 1) // 2, o, j],
            recv_sem=z_recv.at[o, j],
            device_id={"replica": me + direction},
            device_id_type=MESH,
        )

    def sib_copy(o, j, k):
        return pltpu.make_async_remote_copy(
            src_ref=piece(o, j, k),
            dst_ref=piece(o, j, k),
            send_sem=sib_send.at[o, j],
            recv_sem=sib_recv.at[o, j],
            device_id={"sub": 1 - core},
            device_id_type=MESH,
        )

    def xu_copy(o, p):
        return pltpu.make_async_remote_copy(
            src_ref=piece(o, 0, core),
            dst_ref=piece(o, 0, core),
            send_sem=xu_send.at[o, p],
            recv_sem=xu_recv.at[o, t - p],
            device_id={"tensor": peer(p)},
            device_id_type=MESH,
        )

    def xu_arrival(o, p, k, send, recv):
        where = pu.at[peer(p), slab(o), u_cols(k)]
        return pltpu.make_async_remote_copy(
            src_ref=where,
            dst_ref=where,
            send_sem=send.at[o, p],
            recv_sem=recv.at[o, p],
            device_id={"sub": 1 - core},
            device_id_type=MESH,
        )

    def b_cols(i):
        return pl.ds(pl.multiple_of(i * tile, 128), tile)

    def xb_copy(i, p, owner):
        return pltpu.make_async_remote_copy(
            src_ref=xb.at[owner, :, b_cols(i)],
            dst_ref=xb.at[owner, :, b_cols(i)],
            send_sem=xb_send.at[i, p],
            recv_sem=xb_recv.at[i, t - p],
            device_id={"tensor": peer(p)},
            device_id_type=MESH,
        )

    def xr_copy(s, p, owner):
        return pltpu.make_async_remote_copy(
            src_ref=xr.at[s, owner],
            dst_ref=xr.at[s, owner],
            send_sem=xr_send.at[s, p],
            recv_sem=xr_recv.at[s, t - p],
            device_id={"tensor": peer(p)},
            device_id_type=MESH,
        )

    def trade_copy(k, src, dst, direction):
        return pltpu.make_async_remote_copy(
            src_ref=src,
            dst_ref=dst,
            send_sem=trade_send.at[k],
            recv_sem=trade_recv.at[k],
            device_id={"replica": me + direction},
            device_id_type=MESH,
        )

    def rows_copy():
        return trade_copy(0, rows_out, rows_in.at[pl.ds(0, rows_out.shape[0])], inward)

    def tags_copy():
        return trade_copy(1, tags_out, tags_in, inward)

    def back_copy():
        return trade_copy(2, back_out, back_in, outward)

    def w_copy(i):
        return pltpu.make_async_copy(weight.at[:, b_cols(i)], w_v.at[:, b_cols(i)], w_sem.at[i])

    barrier = pltpu.get_barrier_semaphore()

    def greet(device):
        pl.semaphore_signal(barrier, inc=1, device_id=device, device_id_type=MESH)

    act_copy = pltpu.make_async_copy(act, act_v, loc_sem.at[0])
    down_copy = pltpu.make_async_copy(down, pd.at[me], loc_sem.at[1])
    up_copy = pltpu.make_async_copy(up, pu.at[mx, slab(me)], loc_sem.at[2])
    greet({"sub": 1 - core})
    for p in range(1, t):
        greet({"tensor": peer(p)})
    pl.when(me > 0)(lambda: greet({"replica": me - 1}))
    pl.when(me < n - 1)(lambda: greet({"replica": me + 1}))
    act_copy.start()
    down_copy.start()
    up_copy.start()
    order = [lax.rem((mx + 1) * (span // tile) + i, tiles) for i in range(tiles)]
    for i in order:
        w_copy(i).start()
    ends = (me == 0).astype(jnp.int32) + (me == n - 1).astype(jnp.int32)
    pl.semaphore_wait(barrier, t + 2 - ends)

    def on_line(o):
        return (o >= 0) & (o < n)

    def own_send(direction, j, act_on):
        to = me + direction
        wanted = on_line(to)
        if trade and j > 0:
            wanted = wanted & (to > 0) & (to < n - 1)
        pl.when(wanted)(lambda: act_on(z_copy(direction, me, j, True)))

    def own_sends(js, act_on):
        for j in js:
            for direction in (-1, 1):
                own_send(direction, j, act_on)

    early = 1 + PARTS // 2
    own_sends(range(early), lambda c: c.start())
    pl.when(jnp.logical_not(is_end))(
        lambda: own_sends(range(early, pieces), lambda c: c.start())
    )

    act_copy.wait()

    row_voice = voice[...]

    def slot_step(v, slot):
        return jnp.where(row_voice == v, table[v], slot)

    slot_v[...] = lax.fori_loop(0, table.shape[0], slot_step, jnp.zeros_like(row_voice))
    section = lax.broadcasted_iota(jnp.int32, (panel, rows), 0) // rank

    def mask_of(o):
        return section == (slot_v[...] - o * voices)

    def fold(kept):
        return kept.reshape(voices, rank, kept.shape[1]).sum(axis=0)

    def nt_dot(a, b):
        return lax.dot_general(a, b, (((1,), (1,)), ((), ())), preferred_element_type=F32)

    def tn_dot(a, b):
        return lax.dot_general(a, b, (((0,), (0,)), ((), ())), preferred_element_type=F32)

    def send_rank(s):
        for p in range(1, t):
            xr_copy(s, p, mx).start()

    def rank_sum(s):
        for p in range(1, t):
            xr_copy(s, p, peer(p)).wait_recv()
        acc = xr[s, 0]
        for x in range(1, t):
            acc = acc + xr[s, x]
        return (DELTA_GAIN * acc.astype(BF16).astype(F32)).astype(BF16)

    def widen(o, narrowed):
        return jnp.where(mask_of(o), jnp.tile(narrowed, (voices, 1)), jnp.zeros((), BF16))

    def both(s, act_on):
        pl.when(me - s >= 0)(lambda: act_on(me - s, 1))
        pl.when(me + s < n)(lambda: act_on(me + s, -1))

    def take(s, j):
        def one(o, direction):
            z_copy(direction, o, j).wait_recv()
            pl.when(on_line(me + direction))(lambda: z_copy(direction, o, j).start())
            sib_copy(o, j, core).start()
            if j == 0:
                for p in range(1, t):
                    xu_copy(o, p).start()

        both(s, one)

    def process(s, j):
        def one(o, direction):
            side = (direction + 1) // 2
            sib_copy(o, j, 1 - core).wait_recv()
            got = nt_dot(pd[o, :, d_cols(0, j)], act_v[:, d_cols(0, j)])
            got = got + nt_dot(pd[o, :, d_cols(1, j)], act_v[:, d_cols(1, j)])
            if j > 1:
                got = got + made_v[side]
            if j < PARTS:
                made_v[side] = got
            else:
                xr[s, mx] += fold(jnp.where(mask_of(o), got, 0.0))

        both(s, one)

    def relay(o):
        for p in range(1, t):
            xu_arrival(o, p, core, xu_send, xu_recv).wait_recv()
            xu_arrival(o, p, core, sx_send, sx_recv).start()

    def settle_owner(o, narrowed):
        wide = widen(o, narrowed)
        sib_copy(o, 0, 1 - core).wait_recv()
        for p in range(1, t):
            xu_arrival(o, p, 1 - core, sx_send, sx_recv).wait_recv()
        for x in range(t):
            total[:, x * span : (x + 1) * span] += tn_dot(wide, pu[x, slab(o)])

    def settle(s):
        both(s, lambda o, direction: relay(o))
        if trade:
            pl.when(is_end & (s == 2))(lambda: relay(me + inward))
        narrowed = rank_sum(s)
        both(s, lambda o, direction: settle_owner(o, narrowed))
        if trade:
            pl.when(is_end & (s == 2))(lambda: settle_owner(me + inward, narrowed))

    def busy(s):
        some = on_line(me - s) | on_line(me + s)
        if trade:
            some = some & jnp.logical_not(is_end & (s == 1))
        return some

    down_copy.wait()
    xr[0, mx] = fold(jnp.where(mask_of(me), nt_dot(pd[me], act_v[...]), 0.0))
    send_rank(0)
    up_copy.wait()

    def base_tile(i, extra=None):
        w_copy(i).wait()
        part = jnp.dot(act_v[...], w_v[:, b_cols(i)], preferred_element_type=F32)
        if extra is not None:
            part = part + extra
        xb[mx, :, b_cols(i)] = part.astype(BF16)
        for p in range(1, t):
            xb_copy(i, p, mx).start()

    def early_take(j):
        if j == 0 or not trade:
            take(1, j)
        else:
            pl.when(jnp.logical_not(is_end))(lambda: take(1, j))

    others = tiles - span // tile
    for k in range(others):
        base_tile(order[k])
        early_take(k)

    if trade:

        @pl.when(is_end)
        def _():
            target = me + inward
            local_slot = slot_v[...] - target * voices
            chosen = (local_slot >= 0) & (local_slot < voices)
            ones = chosen.astype(F32)
            up_to = lax.broadcasted_iota(jnp.int32, (rows, rows), 0) <= lax.broadcasted_iota(
                jnp.int32, (rows, rows), 1
            )
            counted = jnp.dot(
                jnp.broadcast_to(ones, (8, rows)).astype(BF16),
                up_to.astype(F32).astype(BF16),
                preferred_element_type=F32,
            )[0:1]
            place = lax.broadcasted_iota(jnp.int32, (lanes, rows), 0).astype(F32) + 1.0
            perm = jnp.where((place == counted) & chosen, 1.0, 0.0)
            perm_v[...] = perm
            picked = perm.astype(BF16)
            rows_out[...] = jnp.dot(
                picked[: rows_out.shape[0]], act_v[...], preferred_element_type=F32
            ).astype(BF16)
            tag = jnp.where(chosen, local_slot + 1, 0).astype(F32)
            tags_out[...] = nt_dot(jnp.broadcast_to(tag, (8, rows)).astype(BF16), picked)
            tags_copy().start()
            rows_copy().start()
            own_sends(range(early, pieces), lambda c: c.start())

    wide0 = widen(me, rank_sum(0))
    per = span // tile
    for k in range(per):
        cols = pl.ds(k * tile, tile)
        base_tile(order[others + k], tn_dot(wide0, pu[mx, slab(me), cols]))
        if others + k < pieces:
            early_take(others + k)
    for j in range(tiles, pieces):
        early_take(j)
    total[...] = jnp.zeros_like(total)

    @pl.when(busy(1))
    def _():
        xr[1, mx] = jnp.zeros((rank, rows), F32)
        for j in range(1, pieces):
            process(1, j)
        send_rank(1)

    def serve():
        rows_copy().wait_recv()
        tags_copy().wait_recv()
        got = nt_dot(pd[me], rows_in[...])
        voice_of = (lax.broadcasted_iota(jnp.int32, (panel, lanes), 0) // rank).astype(F32)
        back_out[...] = fold(jnp.where(voice_of + 1.0 == tags_in[0:1], got, 0.0))
        back_copy().start()

    def step(s, carry):
        xr[s, mx] = jnp.zeros((rank, rows), F32)
        for j in range(pieces):
            take(s, j)
            if j > 1:
                process(s, j - 1)
            if trade and j == early - 1:
                pl.when(is_host & (s == 2))(serve)
        process(s, PARTS)
        if trade:

            @pl.when(is_end & (s == 2))
            def _():
                back_copy().wait_recv()
                xr[s, mx] += jnp.dot(
                    back_in[...],
                    perm_v[...],
                    precision=lax.Precision.HIGHEST,
                    preferred_element_type=F32,
                )

        pl.when(busy(s))(lambda: send_rank(s))
        pl.when(busy(s - 1))(lambda: settle(s - 1))
        return carry

    if trade:
        keep = lanes - rows_out.shape[0]
        if keep:
            rows_in[rows_out.shape[0] :] = jnp.zeros((keep, feat), BF16)
    lax.fori_loop(2, n, step, 0)
    pl.when(busy(n - 1))(lambda: settle(n - 1))

    def base_wait(i, carry):
        for p in range(1, t):
            xb_copy(i, p, peer(p)).wait_recv()
        acc = total[:, b_cols(i)]
        for x in range(t):
            acc = acc + xb[x, :, b_cols(i)].astype(F32)
        out[:, b_cols(i)] = acc.astype(BF16)
        for p in range(1, t):
            xb_copy(i, p, mx).wait_send()
        return carry

    lax.fori_loop(0, tiles, base_wait, 0)

    own_sends(range(pieces), lambda c: c.wait_send())
    for p in range(1, t):
        xr_copy(0, p, mx).wait_send()
    if trade:

        @pl.when(is_end)
        def _():
            rows_copy().wait_send()
            tags_copy().wait_send()

        pl.when(is_host)(lambda: back_copy().wait_send())

    def drain(s, carry):
        def sent(o, direction):
            for j in range(pieces):

                def one():
                    pl.when(on_line(me + direction))(lambda: z_copy(direction, o, j).wait_send())
                    sib_copy(o, j, core).wait_send()

                if j == 0 or not trade:
                    one()
                else:
                    pl.when(jnp.logical_not(is_end & (s == 1)))(one)
            for p in range(1, t):
                xu_copy(o, p).wait_send()
                xu_arrival(o, p, core, sx_send, sx_recv).wait_send()

        both(s, sent)

        @pl.when(busy(s))
        def _():
            for p in range(1, t):
                xr_copy(s, p, mx).wait_send()

        return carry

    lax.fori_loop(1, n, drain, 0)


def local(n, t, activations, row_voice, slot_table, weight, down, up):
    rows, feat = activations.shape
    voices, rank, span = up.shape
    width = weight.shape[1]
    panel = voices * rank
    tiles = width // min(TILE, span)
    cap = max(2, rows // min(n, 8))
    sent_rows = -(-cap // 16) * 16
    lanes = -(-cap // 128) * 128
    any_spec = pl.BlockSpec(memory_space=pl.ANY)
    dma = pltpu.SemaphoreType.DMA
    return pl.pallas_call(
        functools.partial(kernel, n, t, voices, rank, cap),
        out_shape=jax.ShapeDtypeStruct((rows, width), BF16),
        in_specs=[
            pl.BlockSpec(memory_space=pltpu.VMEM),
            pl.BlockSpec(memory_space=pltpu.SMEM),
            any_spec,
            any_spec,
            any_spec,
            any_spec,
        ],
        out_specs=pl.BlockSpec(memory_space=pltpu.VMEM),
        scratch_shapes=[
            pltpu.VMEM((rows, feat), BF16),
            pltpu.VMEM((feat, width), BF16),
            pltpu.VMEM((n, panel, feat), BF16),
            pltpu.VMEM((t, n * panel, span), BF16),
            pltpu.VMEM((t, rows, width), BF16),
            pltpu.VMEM((rows, width), F32),
            pltpu.VMEM((n, t, rank, rows), F32),
            pltpu.VMEM((1, rows), jnp.int32),
            pltpu.VMEM((2, panel, rows), F32),
            pltpu.VMEM((lanes, rows), F32),
            pltpu.VMEM((sent_rows, feat), BF16),
            pltpu.VMEM((8, lanes), F32),
            pltpu.VMEM((lanes, feat), BF16),
            pltpu.VMEM((8, lanes), F32),
            pltpu.VMEM((rank, lanes), F32),
            pltpu.VMEM((rank, lanes), F32),
            dma((2, n, PARTS + 1)),
            dma((n, PARTS + 1)),
            dma((n, PARTS + 1)),
            dma((n, PARTS + 1)),
            dma((n, t)),
            dma((n, t)),
            dma((n, t)),
            dma((n, t)),
            dma((tiles, t)),
            dma((tiles, t)),
            dma((n, t)),
            dma((n, t)),
            dma((tiles,)),
            dma((3,)),
            dma((3,)),
            dma((3,)),
        ],
        compiler_params=pltpu.CompilerParams(
            collective_id=0, has_side_effects=True, vmem_limit_bytes=56 * 1024 * 1024
        ),
    )(
        row_voice.reshape(1, rows),
        slot_table,
        activations,
        weight,
        down.reshape(panel, feat),
        up.reshape(panel, span),
    )


def solution(mesh):
    in_specs = (
        P(("groups", "replica", "sub"), "tensor"),
        P(("groups", "replica", "sub")),
        P("groups"),
        P("tensor", None),
        P(("groups", "replica"), None, "tensor"),
        P(("groups", "replica"), None, "tensor"),
    )
    out_specs = P(("groups", "replica", "sub"), None)
    body = functools.partial(local, mesh.shape["replica"], mesh.shape["tensor"])
    return jax.shard_map(body, mesh=mesh, in_specs=in_specs, out_specs=out_specs, check_vma=False)
```

time: 52.9 us -> 52.3 us (0.989)
  no operation moved by 1% of the time
where the time goes in v2:
time: 52.3 us; the launch traced here: 51.9 us
  Pallas kernels  48.6 us (93%)
  local copies, waits for them, and re-layouts  3.31 us (6%)
    pallas_call x1, Pallas kernels, local(): pl.pallas_call(functools.partial(kernel, n, t, voices, rank, cap), out_sh...  48.6 us
    unnamed x1, local copies, waits for them, and re-layouts  2.06 us
    reshape x1, local copies, waits for them, and re-layouts, local(): row_voice.reshape(1, rows)  1.24 us

profile of v2, /device:TPU:0, one launch (start us, length us, event | category | flops | bytes accessed | tf_op | source)
XLA Modules:
  0.0 51.9 jit_solution(13716262024084066709)
XLA Ops:
  0.0 1.2 %reshape.9.voice = s32[1,384]{1,0:T(1,128)} reshape(s32[384]{0:T(512)} %param.7) | data formatting | bytes 3072 | tf_op jit(solution)/shard_map/reshape | solution.py:554
  1.2 48.6 %shard_map.64 = bf16[384,1024]{1,0:T(8,128)(2,1)} custom-call(s32[1,384]{1,0:T(1,128)} %reshape.9.voice, s32[52]{0:T(128)} %table.1, bf16[384,2048]{1,0:T(8,128)(2,1)} %act.1, bf16[2048,1024]{1,0:T(8,128)(2,1)} %weight.1, bf16[208,2048]{1,0:T(8,128)(2,1)} %bitcast.2, bf16[208,512]{1,0:T(8,128)(2,1)} %bitcast.3), custom_call_target="tpu_custom_call" | custom-call | tf_op jit(solution)/shard_map/pallas_call | solution.py:504
  49.9 2.1 %copy.8 = bf16[384,1024]{1,0:T(8,128)(2,1)} copy(bf16[384,1024]{1,0:T(8,128)(2,1)} %shard_map.64) | data formatting | bytes 1572864

commit v3 on v2

--- a/solution.py
+++ b/solution.py
@@ -224,15 +224,11 @@
             for direction in (-1, 1):
                 own_send(direction, j, act_on)
 
-    early = 1 + PARTS // 2
-    own_sends(range(early), lambda c: c.start())
-    pl.when(jnp.logical_not(is_end))(
-        lambda: own_sends(range(early, pieces), lambda c: c.start())
-    )
+    own_sends(range(pieces), lambda c: c.start())
 
     act_copy.wait()
 
-    row_voice = voice[...]
+    row_voice = voice[...].reshape(1, rows)
 
     def slot_step(v, slot):
         return jnp.where(row_voice == v, table[v], slot)
@@ -377,7 +373,6 @@
             tags_out[...] = nt_dot(jnp.broadcast_to(tag, (8, rows)).astype(BF16), picked)
             tags_copy().start()
             rows_copy().start()
-            own_sends(range(early, pieces), lambda c: c.start())
 
     wide0 = widen(me, rank_sum(0))
     per = span // tile
@@ -411,7 +406,7 @@
             take(s, j)
             if j > 1:
                 process(s, j - 1)
-            if trade and j == early - 1:
+            if trade and j == 2:
                 pl.when(is_host & (s == 2))(serve)
         process(s, PARTS)
         if trade:
@@ -551,7 +546,7 @@
             collective_id=0, has_side_effects=True, vmem_limit_bytes=56 * 1024 * 1024
         ),
     )(
-        row_voice.reshape(1, rows),
+        row_voice,
         slot_table,
         activations,
         weight,

time: 52.3 us -> 44.2 us (0.85)
  Pallas kernels: 48.6 us -> 41.8 us
  local copies, waits for them, and re-layouts: 3.31 us -> 2.06 us
    pallas_call x1, Pallas kernels: 48.6 us -> 41.8 us  [local(): pl.pallas_call(functools.partial(kernel, n, t, voices, rank, cap), out_sh...]
    reshape x1 -> x0, local copies, waits for them, and re-layouts: 1.24 us -> none  [local(): row_voice.reshape(1, rows)]
where the time goes in v3:
time: 44.2 us; the launch traced here: 43.9 us
  Pallas kernels  41.8 us (95%)
  local copies, waits for them, and re-layouts  2.06 us (5%)
    pallas_call x1, Pallas kernels, local(): pl.pallas_call(functools.partial(kernel, n, t, voices, rank, cap), out_sh...  41.8 us
    unnamed x1, local copies, waits for them, and re-layouts  2.06 us

profile of v3, /device:TPU:0, one launch (start us, length us, event | category | flops | bytes accessed | tf_op | source)
XLA Modules:
  0.0 43.9 jit_solution(5654335610556476550)
XLA Ops:
  0.0 41.8 %shard_map.64 = bf16[384,1024]{1,0:T(8,128)(2,1)} custom-call(s32[384]{0:T(512)} %voice.1, s32[52]{0:T(128)} %table.1, bf16[384,2048]{1,0:T(8,128)(2,1)} %act.1, bf16[2048,1024]{1,0:T(8,128)(2,1)} %weight.1, bf16[208,2048]{1,0:T(8,128)(2,1)} %bitcast.2, bf16[208,512]{1,0:T(8,128)(2,1)} %bitcast.3), custom_call_target="tpu_custom_call" | custom-call | tf_op jit(solution)/shard_map/pallas_call | solution.py:499
  41.8 2.1 %copy.8 = bf16[384,1024]{1,0:T(8,128)(2,1)} copy(bf16[384,1024]{1,0:T(8,128)(2,1)} %shard_map.64) | data formatting | bytes 1572864

commit v4 on v3

--- a/solution.py
+++ b/solution.py
@@ -498,7 +498,7 @@
     dma = pltpu.SemaphoreType.DMA
     return pl.pallas_call(
         functools.partial(kernel, n, t, voices, rank, cap),
-        out_shape=jax.ShapeDtypeStruct((rows, width), BF16),
+        out_shape=pltpu.VMEM((rows, width), BF16),
         in_specs=[
             pl.BlockSpec(memory_space=pltpu.VMEM),
             pl.BlockSpec(memory_space=pltpu.SMEM),

time: 44.2 us -> 42.2 us (0.955)
  local copies, waits for them, and re-layouts: 2.06 us -> 0.88 us
  Pallas kernels: 41.8 us -> 40.9 us
    unnamed x1, local copies, waits for them, and re-layouts: 2.06 us -> 0.88 us
    pallas_call x1, Pallas kernels: 41.8 us -> 40.9 us  [local(): pl.pallas_call(functools.partial(kernel, n, t, voices, rank, cap), out_sh...]
where the time goes in v4:
time: 42.2 us; the launch traced here: 41.8 us
  Pallas kernels  40.9 us (97%)
  local copies, waits for them, and re-layouts  0.88 us (2%)
    pallas_call x1, Pallas kernels, local(): pl.pallas_call(functools.partial(kernel, n, t, voices, rank, cap), out_sh...  40.9 us
    unnamed x1, local copies, waits for them, and re-layouts  0.88 us

profile of v4, /device:TPU:0, one launch (start us, length us, event | category | flops | bytes accessed | tf_op | source)
XLA Modules:
  0.0 41.8 jit_solution(7187497092012941711)
XLA Ops:
  0.0 40.9 %shard_map.64 = bf16[384,1024]{1,0:T(8,128)(2,1)S(1)} custom-call(s32[384]{0:T(512)} %voice.1, s32[52]{0:T(128)} %table.1, bf16[384,2048]{1,0:T(8,128)(2,1)} %act.1, bf16[2048,1024]{1,0:T(8,128)(2,1)} %weight.1, bf16[208,2048]{1,0:T(8,128)(2,1)} %bitcast.2, bf16[208,512]{1,0:T(8,128)(2,1)} %bitcast.3), custom_call_target="tpu_custom_call" | custom-call | tf_op jit(solution)/shard_map/pallas_call | solution.py:499
  40.9 0.9 %copy.8 = bf16[384,1024]{1,0:T(8,128)(2,1)} copy(bf16[384,1024]{1,0:T(8,128)(2,1)S(1)} %shard_map.64) | data formatting | bytes 1572864

commit v5 on v4

--- a/solution.py
+++ b/solution.py
@@ -430,7 +430,6 @@
         if keep:
             rows_in[rows_out.shape[0] :] = jnp.zeros((keep, feat), BF16)
     lax.fori_loop(2, n, step, 0)
-    pl.when(busy(n - 1))(lambda: settle(n - 1))
 
     def base_wait(i, carry):
         for p in range(1, t):
@@ -438,12 +437,14 @@
         acc = total[:, b_cols(i)]
         for x in range(t):
             acc = acc + xb[x, :, b_cols(i)].astype(F32)
-        out[:, b_cols(i)] = acc.astype(BF16)
+        total[:, b_cols(i)] = acc
         for p in range(1, t):
             xb_copy(i, p, mx).wait_send()
         return carry
 
     lax.fori_loop(0, tiles, base_wait, 0)
+    pl.when(busy(n - 1))(lambda: settle(n - 1))
+    out[...] = total[...].astype(BF16)
 
     own_sends(range(pieces), lambda c: c.wait_send())
     for p in range(1, t):

time: 42.2 us -> 42.3 us (level)
  no operation moved by 1% of the time
where the time goes in v5:
time: 42.3 us; the launch traced here: 41.6 us
  Pallas kernels  40.7 us (96%)
  local copies, waits for them, and re-layouts  0.88 us (2%)
    pallas_call x1, Pallas kernels, local(): pl.pallas_call(functools.partial(kernel, n, t, voices, rank, cap), out_sh...  40.7 us
    unnamed x1, local copies, waits for them, and re-layouts  0.88 us

profile of v5, /device:TPU:0, one launch (start us, length us, event | category | flops | bytes accessed | tf_op | source)
XLA Modules:
  0.0 41.6 jit_solution(13736444719163290627)
XLA Ops:
  0.0 40.7 %shard_map.64 = bf16[384,1024]{1,0:T(8,128)(2,1)S(1)} custom-call(s32[384]{0:T(512)} %voice.1, s32[52]{0:T(128)} %table.1, bf16[384,2048]{1,0:T(8,128)(2,1)} %act.1, bf16[2048,1024]{1,0:T(8,128)(2,1)} %weight.1, bf16[208,2048]{1,0:T(8,128)(2,1)} %bitcast.2, bf16[208,512]{1,0:T(8,128)(2,1)} %bitcast.3), custom_call_target="tpu_custom_call" | custom-call | tf_op jit(solution)/shard_map/pallas_call | solution.py:500
  40.7 0.9 %copy.8 = bf16[384,1024]{1,0:T(8,128)(2,1)} copy(bf16[384,1024]{1,0:T(8,128)(2,1)S(1)} %shard_map.64) | data formatting | bytes 1572864
